TPU v7x, 32 devices: a whole 2x2x4 slice. The times are simulated.
32 devices in a mesh: tm: 16 (over z, y, x), chan: 2 (over core).
Axes of the slice: x: 2, y: 2, z: 4, core: 2. Of those that a mesh axis runs over, the one named last changes fastest.
Arguments:
- strain: bfloat16 [128, 131072], P('chan', 'tm'), as said below
- fir_taps: float32 [128, 64], P('chan'), may hold values from -0.75 to 0.75
Outputs:
- factor: float32 [1024, 1024], P(('tm', 'chan'))
- whitened: bfloat16 [1024, 16384], P(None, ('tm', 'chan'))
Inputs may be any that keep to these rules, and one draw needn't show every extreme that they name: strain-rate samples of 128 channels.
All inputs are finite; a program needn't handle non-finite values.
Results may differ from a plain program's by a relative error of at most 0.001.
The roundings to bfloat16 on the way count: a program that leaves them out, or rounds other values in their place, can miss the bound.
Values may be sent and summed in bfloat16 or wider, within the bound.
A program may use at most 128 MiB of HBM per device.

v0:
```python
import jax
import jax.numpy as jnp
from jax import lax
from jax.sharding import PartitionSpec as P

LAGS = 8
TAPS = 64
STRIDE = 8


def shifted(value, axis, steps):
    count = lax.axis_size(axis)
    initial, last = (max(0, -steps), min(count, count - steps))
    return lax.ppermute(value, axis, [(source, source + steps) for source in range(initial, last)])


def decimate(extended, fir_taps, out_rows):
    channels = extended.shape[0]
    phases = jnp.transpose(extended.astype(jnp.float32).reshape(channels, -1, STRIDE), (0, 2, 1))
    running = jnp.zeros((channels, out_rows), jnp.float32)
    for j in range(TAPS // STRIDE):
        window = phases[:, :, j : j + out_rows]
        weights = fir_taps[:, j * STRIDE : (j + 1) * STRIDE]
        running = running + jnp.einsum(
            "csn,cs->cn", window, weights, precision=lax.Precision.HIGHEST
        )
    return running


def inner_gram(left_rows, right_rows):
    return lax.dot_general(
        left_rows, right_rows, (((1,), (1,)), ((), ())), preferred_element_type=jnp.float32
    )


def local(strain, fir_taps):
    samples = strain.shape[1]
    out_rows = samples // STRIDE
    rim_len = TAPS - STRIDE
    rim_raw = shifted(strain[:, :rim_len], "tm", -1)
    extended = jnp.concatenate([strain, rim_raw], axis=1)
    local_rows = decimate(extended, fir_taps, out_rows).astype(jnp.bfloat16)
    tail_rows = shifted(local_rows[:, : LAGS - 1], "tm", -1)
    decimated = jnp.concatenate([local_rows, tail_rows], axis=1)
    gathered = lax.all_gather(decimated, "chan", axis=0, tiled=True)
    row_count = out_rows // lax.axis_size("chan")
    first_col = lax.axis_index("chan") * row_count
    window = lax.dynamic_slice_in_dim(gathered, first_col, row_count + LAGS - 1, 1)
    hankel = jnp.concatenate([window[:, i : i + row_count] for i in range(LAGS)], axis=0)
    columns = hankel.shape[0]
    gram_full = lax.psum(inner_gram(hankel, hankel), ("tm", "chan"))
    devices_all = lax.axis_size(("tm", "chan"))
    covariance = gram_full / (row_count * devices_all)
    lower_factor = jnp.linalg.cholesky(covariance)
    factor_rows = columns // devices_all
    first_row = lax.axis_index(("tm", "chan")) * factor_rows
    factor_mine = lax.dynamic_slice_in_dim(lower_factor, first_row, factor_rows, 1).T
    whitened = jax.scipy.linalg.solve_triangular(
        lower_factor, hankel.astype(jnp.float32), lower=True
    )
    return (factor_mine, whitened.astype(jnp.bfloat16))


def solution(mesh):
    placed = (P("chan", "tm"), P("chan", None))
    return jax.shard_map(
        local,
        mesh=mesh,
        in_specs=placed,
        out_specs=(P(("tm", "chan"), None), P(None, ("tm", "chan"))),
        check_vma=False,
    )
```

profile of v0, /device:TPU:0, one launch (start us, length us, event | category | flops | bytes accessed | tf_op | source)
XLA Modules:
  0.0 587.2 jit_solution(7478276221011478313)
XLA Ops:
  17.6 5.9 fusion.66
  70.4 5.2 collective-permute-done.1
  82.2 145.1 %all-reduce.3.cloned.1.call-done = f32[1024,1024]{0,1:T(8,128)} async-done(((f32[1024,1024]{0,1:T(8,128)}), f32[1024,1024]{0,1:T(8,128)}) %all-reduce.3.cloned.1.call-update) | async-done | bytes 4194320 | tf_op jit(solution)/shard_map/psum | solution.py:51
  227.4 5.0 broadcast_multiply_fusion
  232.4 5.5 copy.16
  237.9 4.4 fusion
  244.2 11.7 %cholesky.223 = f32[128,128]{1,0:T(8,128)S(1)} custom-call(f32[128,128]{1,0:T(8,128)S(1)} %cholesky.580), custom_call_target="Cholesky" | custom-call | tf_op jit(solution)/shard_map/jit(cholesky)/cholesky | solution.py:54
  256.0 9.8 %custom-call.63 = f32[1,128,128]{1,2,0:T(8,128)S(1)} custom-call(f32[1,128,128]{2,1,0:T(8,128)S(1)} %get-tuple-element.72), custom_call_target="InvertDiagBlocksLowerTriangular" | custom-call | tf_op jit(solution)/shard_map/jit(cholesky)/cholesky | solution.py:54
  271.3 11.9 %cholesky.244 = f32[128,128]{1,0:T(8,128)S(1)} custom-call(f32[128,128]{1,0:T(8,128)S(1)} %cholesky.584), custom_call_target="Cholesky" | custom-call | tf_op jit(solution)/shard_map/jit(cholesky)/cholesky | solution.py:54
  287.2 9.8 %custom-call.64 = f32[1,128,128]{1,2,0:T(8,128)S(1)} custom-call(f32[1,128,128]{2,1,0:T(8,128)S(1)} %get-tuple-element.69), custom_call_target="InvertDiagBlocksLowerTriangular" | custom-call | tf_op jit(solution)/shard_map/jit(cholesky)/cholesky | solution.py:54
  300.4 11.7 %cholesky.468 = f32[128,128]{1,0:T(8,128)S(1)} custom-call(f32[128,128]{1,0:T(8,128)S(1)} %cholesky.589), custom_call_target="Cholesky" | custom-call | tf_op jit(solution)/shard_map/jit(cholesky)/cholesky | solution.py:54
  312.8 9.8 %custom-call.65 = f32[1,128,128]{1,2,0:T(8,128)S(1)} custom-call(f32[1,128,128]{2,1,0:T(8,128)S(1)} %get-tuple-element.66), custom_call_target="InvertDiagBlocksLowerTriangular" | custom-call | tf_op jit(solution)/shard_map/jit(cholesky)/cholesky | solution.py:54
  326.1 12.1 %cholesky.487 = f32[128,128]{1,0:T(8,128)S(1)} custom-call(f32[128,128]{1,0:T(8,128)S(1)} %cholesky.594), custom_call_target="Cholesky" | custom-call | tf_op jit(solution)/shard_map/jit(cholesky)/cholesky | solution.py:54
  338.8 9.8 %custom-call.66 = f32[1,128,128]{1,2,0:T(8,128)S(1)} custom-call(f32[1,128,128]{2,1,0:T(8,128)S(1)} %get-tuple-element.63), custom_call_target="InvertDiagBlocksLowerTriangular" | custom-call | tf_op jit(solution)/shard_map/jit(cholesky)/cholesky | solution.py:54
  352.1 11.7 %cholesky.506 = f32[128,128]{1,0:T(8,128)S(1)} custom-call(f32[128,128]{1,0:T(8,128)S(1)} %cholesky.599), custom_call_target="Cholesky" | custom-call | tf_op jit(solution)/shard_map/jit(cholesky)/cholesky | solution.py:54
  364.5 10.0 %custom-call.67 = f32[1,128,128]{1,2,0:T(8,128)S(1)} custom-call(f32[1,128,128]{2,1,0:T(8,128)S(1)} %get-tuple-element.60), custom_call_target="InvertDiagBlocksLowerTriangular" | custom-call | tf_op jit(solution)/shard_map/jit(cholesky)/cholesky | solution.py:54
  377.7 11.7 %cholesky.526 = f32[128,128]{1,0:T(8,128)S(1)} custom-call(f32[128,128]{1,0:T(8,128)S(1)} %cholesky.604), custom_call_target="Cholesky" | custom-call | tf_op jit(solution)/shard_map/jit(cholesky)/cholesky | solution.py:54
  390.1 9.8 %custom-call.68 = f32[1,128,128]{1,2,0:T(8,128)S(1)} custom-call(f32[1,128,128]{2,1,0:T(8,128)S(1)} %get-tuple-element.57), custom_call_target="InvertDiagBlocksLowerTriangular" | custom-call | tf_op jit(solution)/shard_map/jit(cholesky)/cholesky | solution.py:54
  402.9 11.9 %cholesky.546 = f32[128,128]{1,0:T(8,128)S(1)} custom-call(f32[128,128]{1,0:T(8,128)S(1)} %cholesky.609), custom_call_target="Cholesky" | custom-call | tf_op jit(solution)/shard_map/jit(cholesky)/cholesky | solution.py:54
  415.4 9.8 %custom-call.69 = f32[1,128,128]{1,2,0:T(8,128)S(1)} custom-call(f32[1,128,128]{2,1,0:T(8,128)S(1)} %get-tuple-element.54), custom_call_target="InvertDiagBlocksLowerTriangular" | custom-call | tf_op jit(solution)/shard_map/jit(cholesky)/cholesky | solution.py:54
  427.9 11.7 %cholesky.564 = f32[128,128]{1,0:T(8,128)S(1)} custom-call(f32[128,128]{1,0:T(8,128)S(1)} %convolution_subtract_fusion.13), custom_call_target="Cholesky" | custom-call | tf_op jit(solution)/shard_map/jit(cholesky)/cholesky | solution.py:54
  449.8 4.8 fusion.1
  455.6 27.7 %while.1 = (s32[]{:T(128)}, f32[1024,1024]{1,0:T(8,128)}, s32[8,2]{0,1:T(2,128)S(1)}, f32[8,128,128]{2,1,0:T(8,128)}, s32[]{:T(128)}) while((s32[]{:T(128)}, f32[1024,1024]{1,0:T(8,128)}, s32[8,2]{0,1:T(2,128)S(1)}, f32[8,128,128]{2,1,0:T(8,128)}, s32[]{:T(128)}) %tuple.73), condition=%wide.while_cond, body=%wide.while_body.sunk | while | flops 2 | bytes 132205 | solution.py:58
  483.4 79.6 %custom-call.70 = f32[8,128,128]{1,2,0:T(8,128)S(1)} custom-call(f32[8,128,128]{2,1,0:T(8,128)} %get-tuple-element.9), custom_call_target="InvertDiagBlocksLowerTriangular" | custom-call | tf_op jit(solution)/shard_map/jit(_solve_triangular)/triangular_solve | solution.py:58
  (145 shorter events, 148.3 us)
Async XLA Ops:
  7.2 220.2 %all-reduce.3.cloned.1.call-start = ((), (), s32[]{:S(2)}) async-start(), calls=%async_computation | async-start | bytes 8388608 | tf_op jit(solution)/shard_map/psum | solution.py:51
  7.9 6.5 %collective-permute-start = (bf16[64,56]{1,0:T(8,128)(2,1)S(1)}, bf16[64,56]{1,0:T(8,128)(2,1)S(1)}, u32[]{:S(2)}, u32[]{:S(2)}) collective-permute-start(bf16[64,56]{1,0:T(8,128)(2,1)S(1)} %slice.324), channel_id=1, source_target_pairs={{2,0},{4,2},{6,4},{8,6},{10,8},{12,10},{14,12},{16,14},{18,16},{20... | collective-permute-start | bytes 21512 | tf_op jit(solution)/shard_map/ppermute | solution.py:14
  23.5 12.9 %copy-start.2 = (bf16[64,8,1024]{0,1,2:T(8,128)(2,1)S(1)}, bf16[64,8,1024]{0,1,2:T(8,128)(2,1)}, u32[]{:S(2)}) copy-start(bf16[64,8,1024]{0,1,2:T(8,128)(2,1)} %get-tuple-element.30) | copy-start | bytes 3145732
  39.8 13.0 %copy-start.1 = (bf16[64,8,1024]{0,1,2:T(8,128)(2,1)S(1)}, bf16[64,8,1024]{0,1,2:T(8,128)(2,1)}, u32[]{:S(2)}) copy-start(bf16[64,8,1024]{0,1,2:T(8,128)(2,1)} %get-tuple-element.26) | copy-start | bytes 3145732
  55.8 9.0 %copy-start.5 = (bf16[64,8,1024]{2,1,0:T(8,128)(2,1)S(1)}, bf16[64,8,1024]{2,1,0:T(8,128)(2,1)}, u32[]{:S(2)}) copy-start(bf16[64,8,1024]{2,1,0:T(8,128)(2,1)} %copy.34) | copy-start | bytes 3145732
  55.8 10.0 %copy-start.4 = (bf16[64,8,1024]{2,1,0:T(8,128)(2,1)S(1)}, bf16[64,8,1024]{2,1,0:T(8,128)(2,1)}, u32[]{:S(2)}) copy-start(bf16[64,8,1024]{2,1,0:T(8,128)(2,1)} %copy.31) | copy-start | bytes 3145732
  55.8 10.9 %copy-start.3 = (bf16[64,8,1024]{2,1,0:T(8,128)(2,1)S(1)}, bf16[64,8,1024]{2,1,0:T(8,128)(2,1)}, u32[]{:S(2)}) copy-start(bf16[64,8,1024]{2,1,0:T(8,128)(2,1)} %copy.28) | copy-start | bytes 3145732
  69.1 6.5 %collective-permute-start.1 = (bf16[64,7]{1,0:T(8,128)(2,1)S(1)}, bf16[64,7]{1,0:T(8,128)(2,1)S(1)}, u32[]{:S(2)}, u32[]{:S(2)}) collective-permute-start(bf16[64,7]{1,0:T(8,128)(2,1)S(1)} %slice.369), channel_id=1, source_target_pairs={{2,0},{4,2},{6,4},{8,6},{10,8},{12,10},{14,12},{16,14},{18,16},{20... | collective-permute-start | bytes 2696 | tf_op jit(solution)/shard_map/ppermute | solution.py:14
  242.3 1.9 copy-start
  270.4 26.6 %copy-start.6 = (f32[896,128]{1,0:T(8,128)S(1)}, f32[896,128]{1,0:T(8,128)}, u32[]{:S(2)}) copy-start(f32[896,128]{1,0:T(8,128)} %convolution_subtract_fusion) | copy-start | bytes 1376260
  578.9 1.0 copy-start.7
Sparse Core Ops, SparseCore 0:
  82.1 145.2 all-reduce.2
where the time goes:
time: 596 us; the launch traced here: 587 us
  other arithmetic  268 us (45%)
  waiting for transfers between devices  154 us (26%)
  local copies, waits for them, and re-layouts  84.9 us (14%)
  matrix products  54.8 us (9%)
  between operations  20.1 us (3%)
    another operation x30, other arithmetic, local(): lower_factor = jnp.linalg.cholesky(covariance)  172 us
    psum x1, waiting for transfers between devices, local(): gram_full = lax.psum(inner_gram(hankel, hankel), ('tm', 'chan'))  145 us
    another operation x3, other arithmetic, local(): jax.scipy.linalg.solve_triangular(lower_factor, hankel.astype(jnp.float32...  84.5 us
    slice x9, local copies, waits for them, and re-layouts, decimate(): window = phases[:, :, j:j + out_rows]  38.1 us
    another operation x24, local copies, waits for them, and re-layouts  27.7 us
    another operation x14, matrix products, local(): lower_factor = jnp.linalg.cholesky(covariance)  23.5 us
    another operation x15, matrix products, local(): jax.scipy.linalg.solve_triangular(lower_factor, hankel.astype(jnp.float32...  15.2 us
    dot_general x8, matrix products, decimate(): jnp.einsum('csn,cs->cn', window, weights, precision=lax.Precision.HIGHEST)  12.8 us
  transfers between devices with their start and end apart: 3, of which 3 were waited for; matrix products, arithmetic and copies ran while one was open for 0% of the time, Pallas kernels for 0%

commit v1 on v0

v1 whole, which is shorter than its diff:
```python
import functools

import jax
import jax.numpy as jnp
from jax import lax
from jax.experimental import pallas as pl
from jax.experimental.pallas import tpu as pltpu
from jax.sharding import PartitionSpec as P

LAGS = 8
TAPS = 64
STRIDE = 8
LANES = 128
HIGHEST = lax.Precision.HIGHEST
VMEM = pl.BlockSpec(memory_space=pltpu.VMEM)


def shifted(value, axis, steps):
    count = lax.axis_size(axis)
    initial, last = (max(0, -steps), min(count, count - steps))
    return lax.ppermute(value, axis, [(source, source + steps) for source in range(initial, last)])


def decimate_kernel(strain_ref, rim_ref, taps_ref, out_ref, phase_ref):
    channels, samples = strain_ref.shape
    out_rows = samples // STRIDE
    width = STRIDE * LANES
    sample = lax.broadcasted_iota(jnp.int32, (width, width), 0)
    column = lax.broadcasted_iota(jnp.int32, (width, width), 1)
    wanted = STRIDE * (column % LANES) + column // LANES
    select = jnp.where(sample == wanted, 1.0, 0.0).astype(jnp.bfloat16)
    for g in range(out_rows // LANES + 1):
        if g < out_rows // LANES:
            part = jnp.dot(strain_ref[:, g * width : (g + 1) * width], select, preferred_element_type=jnp.float32)
        else:
            part = jnp.dot(rim_ref[...], select[:LANES], preferred_element_type=jnp.float32)
        for s in range(STRIDE):
            phase_ref[s, :, g * LANES : (g + 1) * LANES] = part[:, s * LANES : (s + 1) * LANES]
    span = out_rows + LANES
    for c in range(0, channels, 16):
        rows = slice(c, c + 16)
        total = jnp.zeros((16, span), jnp.float32)
        for j in range(TAPS // STRIDE):
            term = jnp.zeros((16, span), jnp.float32)
            for s in range(STRIDE):
                k = j * STRIDE + s
                term += taps_ref[rows, k : k + 1] * phase_ref[s, rows, :]
            total += term if j == 0 else pltpu.roll(term, span - j, 1)
        out_ref[rows, :] = total.astype(jnp.bfloat16)


def decimate(strain, rim, taps):
    channels, samples = strain.shape
    span = samples // STRIDE + LANES
    return pl.pallas_call(
        decimate_kernel,
        out_shape=jax.ShapeDtypeStruct((channels, span), jnp.bfloat16),
        in_specs=[VMEM] * 3,
        out_specs=VMEM,
        scratch_shapes=[pltpu.VMEM((STRIDE, channels, span), jnp.float32)],
        compiler_params=pltpu.CompilerParams(vmem_limit_bytes=40 * 2**20),
    )(strain, rim, taps)


def hankel_kernel(rows_ref, hankel_ref, sums_ref):
    group, first = lax.axis_index("tm"), lax.axis_index("chan")
    channels = rows_ref.shape[0]
    count = hankel_ref.shape[1]
    start = pl.multiple_of(first * count, LANES)
    window = rows_ref[:, pl.ds(start, count + LANES)].astype(jnp.float32)
    span = count + LANES
    for i in range(LAGS):
        moved = window if i == 0 else pltpu.roll(window, span - i, 1)
        hankel_ref[i * channels : (i + 1) * channels, :] = moved[:, :count].astype(jnp.bfloat16)
    leads = jnp.logical_and(group == 0, first == 0)
    skip = jnp.where(leads, LAGS - 1, 0)
    keep = lax.broadcasted_iota(jnp.int32, (channels, count), 1) >= skip
    left = jnp.where(keep, window[:, :count], 0.0).astype(jnp.bfloat16)
    sums_ref[:, : LAGS * channels] = lax.dot_general(
        left, hankel_ref[...], (((1,), (1,)), ((), ())), preferred_element_type=jnp.float32
    )
    lane = lax.broadcasted_iota(jnp.int32, (channels, LANES), 1)
    seen = jnp.where(leads, 2 * LAGS, 0)
    sums_ref[:, LAGS * channels :] = jnp.where(lane < seen, window[:, :LANES], 0.0)


def hankel_and_sums(rows, count):
    channels = rows.shape[0]
    return pl.pallas_call(
        hankel_kernel,
        out_shape=(
            jax.ShapeDtypeStruct((LAGS * channels, count), jnp.bfloat16),
            jax.ShapeDtypeStruct((channels, LAGS * channels + LANES), jnp.float32),
        ),
        in_specs=[VMEM],
        out_specs=(VMEM, VMEM),
        compiler_params=pltpu.CompilerParams(vmem_limit_bytes=40 * 2**20),
    )(rows)


def factor_block(block):
    size = block.shape[0]
    row_id = lax.broadcasted_iota(jnp.int32, (size, size), 0)
    col_id = lax.broadcasted_iota(jnp.int32, (size, size), 1)
    sub = lax.broadcasted_iota(jnp.int32, (8, size), 0)
    low = block
    inv = jnp.where(row_id == col_id, 1.0, 0.0)
    factors, inverses = [], []
    for b in range(size // 8):
        cols = [jnp.broadcast_to(low[:, 8 * b + j : 8 * b + j + 1], low.shape) for j in range(8)]
        top, low = low[:8], low[8:]
        x_top, inv = inv[:8], inv[8:]
        c_top, c_low = [c[:8] for c in cols], [c[8:] for c in cols]
        scale = jnp.zeros((8, size), jnp.float32)
        more = b < size // 8 - 1
        for i in range(8):
            root = lax.rsqrt(jnp.broadcast_to(c_top[i][i : i + 1], (8, size)))
            over = root[:1] * root[:1]
            scale = jnp.where(sub == i, root, scale)
            below = jnp.where(sub > i, c_top[i], 0.0)
            row, x_row = top[i : i + 1] * over, x_top[i : i + 1] * over
            c_row = [c_top[j][i : i + 1] * over for j in range(i + 1, 8)]
            top, x_top = top - below * row, x_top - below * x_row
            for j in range(i + 1, 8):
                c_top[j] = c_top[j] - below * c_row[j - i - 1]
            if more:
                low, inv = low - c_low[i] * row, inv - c_low[i] * x_row
                for j in range(i + 1, 8):
                    c_low[j] = c_low[j] - c_low[i] * c_row[j - i - 1]
        factors.append(top * scale)
        inverses.append(x_top * scale)
    factor = jnp.concatenate(factors, axis=0)
    return jnp.where(col_id >= row_id, factor, 0.0), jnp.concatenate(inverses, axis=0)


def whiten_kernel(rows_all, sums_ref, hankel_ref, factor_ref, white_ref, work_ref):
    columns, count = hankel_ref.shape
    channels = columns // LAGS
    size = channels
    head = sums_ref[:, columns:]
    lane = lax.broadcasted_iota(jnp.int32, (channels, LANES), 1)
    heads = [(head if i == 0 else pltpu.roll(head, LANES - i, 1)).astype(jnp.bfloat16) for i in range(LAGS)]
    head_hankel = jnp.concatenate(heads, axis=0)
    scale = 1.0 / rows_all
    for i in range(LAGS):
        wide = columns - i * channels
        own = jnp.logical_and(lane >= i, lane < LAGS - 1)
        left = jnp.where(own, head, 0.0).astype(jnp.bfloat16)
        extra = lax.dot_general(
            left, head_hankel[:wide], (((1,), (1,)), ((), ())), preferred_element_type=jnp.float32
        )
        work_ref[i * channels : (i + 1) * channels, i * channels : columns] = (sums_ref[:, :wide] + extra) * scale
        if i:
            work_ref[i * channels : (i + 1) * channels, : i * channels] = jnp.zeros((channels, i * channels), jnp.float32)
    work_ref[:, columns:] = hankel_ref[...].astype(jnp.float32)

    def step(k, _):
        first = pl.multiple_of(k * size, size)
        mine = pl.ds(first, size)
        factor, inverse = factor_block(work_ref[mine, mine])
        solved = jnp.dot(inverse, work_ref[mine, :], preferred_element_type=jnp.float32, precision=HIGHEST)
        work_ref[mine, :] = solved
        work_ref[mine, mine] = factor
        white_ref[mine, :] = solved[:, columns:].astype(jnp.bfloat16)

        def update(i, _):
            other = pl.ds(pl.multiple_of(i * size, size), size)
            work_ref[other, :] -= lax.dot_general(
                work_ref[mine, other],
                work_ref[mine, :],
                (((0,), (0,)), ((), ())),
                preferred_element_type=jnp.float32,
                precision=HIGHEST,
            )
            return 0

        lax.fori_loop(k + 1, LAGS, update, 0)
        return 0

    lax.fori_loop(0, LAGS, step, 0)
    kept = factor_ref.shape[0]
    me = lax.axis_index("tm") * lax.axis_size("chan") + lax.axis_index("chan")
    first_row = pl.multiple_of(me * (columns // (lax.axis_size("tm") * lax.axis_size("chan"))) // kept * kept, kept)
    rows = work_ref[pl.ds(first_row, kept), :columns]
    row_id = lax.broadcasted_iota(jnp.int32, rows.shape, 0) + first_row
    col_id = lax.broadcasted_iota(jnp.int32, rows.shape, 1)
    factor_ref[...] = jnp.where(col_id >= row_id, rows, 0.0)


def whiten(sums, hankel, rows_all, kept):
    columns, count = hankel.shape
    return pl.pallas_call(
        functools.partial(whiten_kernel, rows_all),
        out_shape=(
            jax.ShapeDtypeStruct((kept, columns), jnp.float32),
            jax.ShapeDtypeStruct((columns, count), jnp.bfloat16),
        ),
        in_specs=[VMEM, VMEM],
        out_specs=(VMEM, VMEM),
        scratch_shapes=[pltpu.VMEM((columns, columns + count), jnp.float32)],
        compiler_params=pltpu.CompilerParams(vmem_limit_bytes=48 * 2**20),
    )(sums, hankel)


def local(strain, fir_taps):
    samples = strain.shape[1]
    out_rows = samples // STRIDE
    rim = shifted(strain[:, :LANES], "tm", -1)
    decimated = decimate(strain, rim, fir_taps)
    gathered = lax.all_gather(decimated, "chan", axis=0, tiled=True)
    row_count = out_rows // lax.axis_size("chan")
    hankel, sums = hankel_and_sums(gathered, row_count)
    sums = lax.psum(sums, ("tm", "chan"))
    devices_all = lax.axis_size(("tm", "chan"))
    columns = hankel.shape[0]
    factor_rows = columns // devices_all
    kept = max(8, factor_rows)
    factor, whitened = whiten(sums, hankel, row_count * devices_all, kept)
    if kept > factor_rows:
        first_row = lax.axis_index(("tm", "chan")) * factor_rows % kept
        factor = lax.dynamic_slice_in_dim(factor, first_row, factor_rows, 0)
    return (factor, whitened)


def solution(mesh):
    placed = (P("chan", "tm"), P("chan", None))
    return jax.shard_map(
        local,
        mesh=mesh,
        in_specs=placed,
        out_specs=(P(("tm", "chan"), None), P(None, ("tm", "chan"))),
        check_vma=False,
    )
```

time: 596 us -> 232 us (0.39); the launches traced: 587 us -> 232 us
  other arithmetic: 268 us -> 0 us
  local copies, waits for them, and re-layouts: 84.9 us -> 3.01 us
  Pallas kernels: 0 us -> 76 us
  matrix products: 54.8 us -> 0 us
  waiting for transfers between devices: 154 us -> 135 us
  between operations: 20.1 us -> 14.1 us
    another operation x33 -> x0, other arithmetic: 257 us -> none  [the longest x30 172 us: local(): lower_factor = jnp.linalg.cholesky(covariance)]
    pallas_call x0 -> x3, Pallas kernels: none -> 76 us  [the longest x1 70.9 us: whiten(): pl.pallas_call(functools.partial(whiten_kernel, rows_all), out_shape=(jax...]
    slice x12 -> x1, local copies, waits for them, and re-layouts: 40 us -> 0.72 us  [local(): rim = shifted(strain[:, :LANES], 'tm', -1)]
    another operation x29 -> x0, matrix products: 38.7 us -> none  [the longest x14 23.5 us: local(): lower_factor = jnp.linalg.cholesky(covariance)]
    another operation x36 -> x0, local copies, waits for them, and re-layouts: 32.3 us -> none
    dot_general x9 -> x0, matrix products: 16.1 us -> none  [the longest x8 12.8 us: decimate(): jnp.einsum('csn,cs->cn', window, weights, precision=lax.Precision.HIGHEST)]
    psum x1, waiting for transfers between devices: 145 us -> 130 us  [local(): sums = lax.psum(sums, ('tm', 'chan'))]
    div x2 -> x0, other arithmetic: 9.45 us -> none  [the longest x1 5 us: local(): covariance = gram_full / (row_count * devices_all)]
  transfers between devices with their start and end apart: 3 -> 2, of which waited for: 3 -> 2; matrix products, arithmetic and copies ran while one was open for 0% -> 0% of each run, Pallas kernels for 0% -> 0%
where the time goes in v1:
time: 232 us
  waiting for transfers between devices  135 us (58%)
  Pallas kernels  76 us (33%)
  between operations  14.1 us (6%)
  local copies, waits for them, and re-layouts  3.01 us (1%)
    psum x1, waiting for transfers between devices, local(): sums = lax.psum(sums, ('tm', 'chan'))  130 us
    pallas_call x1, Pallas kernels, whiten(): pl.pallas_call(functools.partial(whiten_kernel, rows_all), out_shape=(jax...  70.9 us
    ppermute x1, waiting for transfers between devices, shifted(): lax.ppermute(value, axis, [(source, source + steps) for source in range(i...  5.26 us
  transfers between devices with their start and end apart: 2, of which 2 were waited for; matrix products, arithmetic and copies ran while one was open for 0% of the time, Pallas kernels for 0%

profile of v1, /device:TPU:0, one launch (start us, length us, event | category | flops | bytes accessed | tf_op | source)
XLA Modules:
  0.0 231.6 jit_solution(6389806500213536422)
XLA Ops:
  7.2 0.0 copy-start.2
  7.2 0.0 all-reduce.2.cloned.1.call-start
  7.2 0.7 slice.3
  7.9 1.3 collective-permute-start
  9.2 5.3 %collective-permute-done.rim_ref = bf16[64,128]{1,0:T(8,128)(2,1)S(1)} collective-permute-done((bf16[64,128]{1,0:T(8,128)(2,1)S(1)}, bf16[64,128]{1,0:T(8,128)(2,1)S(1)}, u32[]{:S(2)}, u32[]{:S(2)}) %collective-permute-start) | collective-permute-done | bytes 16416 | tf_op jit(solution)/shard_map/ppermute | solution.py:21
  14.5 0.0 copy-done.2
  14.5 0.0 copy-start
  14.5 1.2 copy-done
  15.7 3.7 %shard_map.41 = bf16[64,1152]{1,0:T(8,128)(2,1)S(1)} custom-call(bf16[64,8192]{1,0:T(8,128)(2,1)S(1)} %copy-done, bf16[64,128]{1,0:T(8,128)(2,1)S(1)} %collective-permute-done.rim_ref, f32[64,64]{1,0:T(8,128)S(1)} %copy-done.2), custom_call_target="tpu_custom_call" | custom-call | tf_op jit(solution)/shard_map/pallas_call | solution.py:55
  19.4 2.0 all_gather.3.rows_ref
  21.4 1.4 shard_map.42
  22.8 0.0 all-reduce.2.cloned.1.call-update
  22.8 130.0 %all-reduce.2.cloned.1.call-done.sums_ref = f32[128,1152]{1,0:T(8,128)} async-done(((f32[128,1152]{1,0:T(8,128)}), f32[128,1152]{1,0:T(8,128)}) %all-reduce.2.cloned.1.call-update) | async-done | bytes 589840 | tf_op jit(solution)/shard_map/psum | solution.py:213
  152.8 0.0 copy-start.1
  152.8 1.1 copy-done.1
  153.9 70.9 %shard_map.43 = (f32[32,1024]{1,0:T(8,128)}, bf16[1024,512]{1,0:T(8,128)(2,1)}) custom-call(f32[128,1152]{1,0:T(8,128)S(1)} %copy-done.1, bf16[1024,512]{1,0:T(8,128)(2,1)S(1)} %get-tuple-element.5.hankel_ref), custom_call_target="tpu_custom_call" | custom-call | tf_op jit(solution)/shard_map/pallas_call | solution.py:192
Async XLA Ops:
  7.2 7.3 %copy-start.2 = (f32[64,64]{1,0:T(8,128)S(1)}, f32[64,64]{1,0:T(8,128)}, u32[]{:S(2)}) copy-start(f32[64,64]{1,0:T(8,128)} %taps_ref.1) | copy-start | bytes 49156
  7.2 145.7 %all-reduce.2.cloned.1.call-start = ((), (), s32[]{:S(2)}) async-start(), calls=%async_computation | async-start | bytes 1179648 | tf_op jit(solution)/shard_map/psum | solution.py:213
  7.9 6.5 %collective-permute-start = (bf16[64,128]{1,0:T(8,128)(2,1)S(1)}, bf16[64,128]{1,0:T(8,128)(2,1)S(1)}, u32[]{:S(2)}, u32[]{:S(2)}) collective-permute-start(bf16[64,128]{1,0:T(8,128)(2,1)S(1)} %slice.3), channel_id=1, source_target_pairs={{2,0},{4,2},{6,4},{8,6},{10,8},{12,10},{14,12},{16,14},{18,16},{20... | collective-permute-start | bytes 49160 | tf_op jit(solution)/shard_map/ppermute | solution.py:21
  14.5 1.2 copy-start
  152.8 1.1 copy-start.1
Sparse Core Ops, SparseCore 0:
  22.9 129.8 all-reduce.1

commit v2 on v1

--- a/solution.py
+++ b/solution.py
@@ -11,6 +11,7 @@
 TAPS = 64
 STRIDE = 8
 LANES = 128
+MESH = pl.DeviceIdType.MESH
 HIGHEST = lax.Precision.HIGHEST
 VMEM = pl.BlockSpec(memory_space=pltpu.VMEM)
 
@@ -96,6 +97,118 @@
         out_specs=(VMEM, VMEM),
         compiler_params=pltpu.CompilerParams(vmem_limit_bytes=40 * 2**20),
     )(rows)
+
+
+def sum_kernel(near, mine_ref, out_ref, total, from_core, from_near, from_far, full, core_sem, near_sem, far_sem, all_sem, hand_sem):
+    tm, chan = lax.axis_index("tm"), lax.axis_index("chan")
+    far = lax.axis_size("tm") // near
+    spot, place = lax.rem(tm, near), lax.div(tm, near)
+    rows = mine_ref.shape[0]
+    half = rows // 2
+    piece = half // near
+    core = {"chan": 1 - chan}
+
+    def near_of(d):
+        return lax.rem(spot + d, near)
+
+    def near_id(d):
+        return {"tm": place * near + near_of(d)}
+
+    def far_id(d):
+        return {"tm": lax.rem(place + d, far) * near + spot}
+
+    def copy(source, target, sems, slot, device):
+        return pltpu.make_async_remote_copy(
+            src_ref=source,
+            dst_ref=target,
+            send_sem=sems.at[0, slot],
+            recv_sem=sems.at[1, slot],
+            device_id=device,
+            device_id_type=MESH,
+        )
+
+    barrier = pltpu.get_barrier_semaphore()
+    partners = [core] + [near_id(d) for d in range(1, near)] + [far_id(d) for d in range(1, far)]
+    for partner in partners:
+        pl.semaphore_signal(barrier, inc=1, device_id=partner, device_id_type=MESH)
+    pl.semaphore_wait(barrier, len(partners))
+
+    away = pl.ds(pl.multiple_of((1 - chan) * half, half), half)
+    home = pl.ds(pl.multiple_of(chan * half, half), half)
+    step = copy(mine_ref.at[away], from_core, core_sem, 0, core)
+    step.start()
+    step.wait()
+    total[...] = mine_ref[home] + from_core[...]
+
+    steps = []
+    for d in range(1, near):
+        part = total.at[pl.ds(pl.multiple_of(near_of(d) * piece, piece), piece)]
+        steps.append(copy(part, from_near.at[d - 1], near_sem, d - 1, near_id(d)))
+        steps[-1].start()
+    own = total[pl.ds(pl.multiple_of(spot * piece, piece), piece)]
+    for d in range(1, near):
+        steps[d - 1].wait()
+        own += from_near[d - 1]
+
+    from_far[place] = own
+    steps = []
+    for d in range(1, far):
+        steps.append(copy(from_far.at[place], from_far.at[place], far_sem, d - 1, far_id(d)))
+        steps[-1].start()
+    for step in steps:
+        step.wait()
+    own = from_far[0]
+    for d in range(1, far):
+        own += from_far[d]
+
+    def at(spot_of):
+        return pl.ds(pl.multiple_of(chan * half + spot_of * piece, piece), piece)
+
+    full[at(spot)] = own
+    steps = []
+    for d in range(1, near):
+        steps.append(copy(full.at[at(spot)], full.at[at(spot)], all_sem, d - 1, near_id(d)))
+        steps[-1].start()
+    hands = [copy(full.at[at(spot)], full.at[at(spot)], hand_sem, 0, core)]
+    hands[0].start()
+    for d in range(1, near):
+        steps[d - 1].wait()
+        came = at(lax.rem(spot - d + near, near))
+        hands.append(copy(full.at[came], full.at[came], hand_sem, d, core))
+        hands[-1].start()
+    for hand in hands:
+        hand.wait()
+    out_ref[...] = full[...]
+
+
+def summed(value):
+    rows, columns = value.shape
+    tm = lax.axis_size("tm")
+    near = 4 if tm % 4 == 0 else 2
+    far = tm // near
+    half, piece = rows // 2, rows // 2 // near
+    dtype = jnp.float32
+    return pl.pallas_call(
+        functools.partial(sum_kernel, near),
+        out_shape=jax.ShapeDtypeStruct((rows, columns), dtype),
+        in_specs=[VMEM],
+        out_specs=VMEM,
+        scratch_shapes=[
+            pltpu.VMEM((half, columns), dtype),
+            pltpu.VMEM((half, columns), dtype),
+            pltpu.VMEM((near - 1, piece, columns), dtype),
+            pltpu.VMEM((far, piece, columns), dtype),
+            pltpu.VMEM((rows, columns), dtype),
+            pltpu.SemaphoreType.DMA((2, 1)),
+            pltpu.SemaphoreType.DMA((2, near - 1)),
+            pltpu.SemaphoreType.DMA((2, max(far - 1, 1))),
+            pltpu.SemaphoreType.DMA((2, near - 1)),
+            pltpu.SemaphoreType.DMA((2, near)),
+        ],
+        compiler_params=pltpu.CompilerParams(
+            collective_id=0, has_side_effects=True, vmem_limit_bytes=24 * 2**20
+        ),
+    )(value)
 
 
 def factor_block(block):
@@ -210,7 +323,7 @@
     gathered = lax.all_gather(decimated, "chan", axis=0, tiled=True)
     row_count = out_rows // lax.axis_size("chan")
     hankel, sums = hankel_and_sums(gathered, row_count)
-    sums = lax.psum(sums, ("tm", "chan"))
+    sums = summed(sums)
     devices_all = lax.axis_size(("tm", "chan"))
     columns = hankel.shape[0]
     factor_rows = columns // devices_all

time: 232 us -> 112 us (0.48)
  waiting for transfers between devices: 135 us -> 5.26 us
  Pallas kernels: 76 us -> 101 us
  between operations: 14.1 us -> 0.67 us
    psum x1 -> x0, waiting for transfers between devices: 130 us -> none  [local(): sums = lax.psum(sums, ('tm', 'chan'))]
    pallas_call x0 -> x1, Pallas kernels: none -> 25.8 us  [summed(): pl.pallas_call(functools.partial(sum_kernel, near), out_shape=jax.ShapeDt...]
  transfers between devices with their start and end apart: 2 -> 1, of which waited for: 2 -> 1; matrix products, arithmetic and copies ran while one was open for 0% -> 0% of each run, Pallas kernels for 0% -> 0%
where the time goes in v2:
time: 112 us
  Pallas kernels  101 us (90%)
  waiting for transfers between devices  5.26 us (5%)
  blocking collectives  2.02 us (2%)
  local copies, waits for them, and re-layouts  1.95 us (2%)
  starting transfers between devices  1.28 us (1%)
    pallas_call x1, Pallas kernels, whiten(): pl.pallas_call(functools.partial(whiten_kernel, rows_all), out_shape=(jax...  70.9 us
    pallas_call x1, Pallas kernels, summed(): pl.pallas_call(functools.partial(sum_kernel, near), out_shape=jax.ShapeDt...  25.8 us
    ppermute x1, waiting for transfers between devices, shifted(): lax.ppermute(value, axis, [(source, source + steps) for source in range(i...  5.26 us
    pallas_call x1, Pallas kernels, decimate(): pl.pallas_call(decimate_kernel, out_shape=jax.ShapeDtypeStruct((channels,...  3.67 us
  transfers between devices with their start and end apart: 1, of which 1 were waited for; matrix products, arithmetic and copies ran while one was open for 0% of the time, Pallas kernels for 0%

profile of v2, /device:TPU:0, one launch (start us, length us, event | category | flops | bytes accessed | tf_op | source)
XLA Modules:
  0.0 112.2 jit_solution(4129921764034968984)
XLA Ops:
  0.6 0.0 copy-start.1
  0.6 0.7 slice.3
  1.4 1.3 %collective-permute-start = (bf16[64,128]{1,0:T(8,128)(2,1)S(1)}, bf16[64,128]{1,0:T(8,128)(2,1)S(1)}, u32[]{:S(2)}, u32[]{:S(2)}) collective-permute-start(bf16[64,128]{1,0:T(8,128)(2,1)S(1)} %slice.3), channel_id=1, source_target_pairs={{2,0},{4,2},{6,4},{8,6},{10,8},{12,10},{14,12},{16,14},{18,16},{20... | collective-permute-start | bytes 49160 | tf_op jit(solution)/shard_map/ppermute | solution.py:22
  2.7 5.3 %collective-permute-done.rim_ref = bf16[64,128]{1,0:T(8,128)(2,1)S(1)} collective-permute-done((bf16[64,128]{1,0:T(8,128)(2,1)S(1)}, bf16[64,128]{1,0:T(8,128)(2,1)S(1)}, u32[]{:S(2)}, u32[]{:S(2)}) %collective-permute-start) | collective-permute-done | bytes 16416 | tf_op jit(solution)/shard_map/ppermute | solution.py:22
  7.9 0.0 copy-done.1
  7.9 0.0 copy-start
  7.9 1.2 %copy-done = bf16[64,8192]{1,0:T(8,128)(2,1)S(1)} copy-done((bf16[64,8192]{1,0:T(8,128)(2,1)S(1)}, bf16[64,8192]{1,0:T(8,128)(2,1)}, u32[]{:S(2)}) %copy-start) | copy-done | bytes 1048600
  9.1 3.7 %shard_map.41 = bf16[64,1152]{1,0:T(8,128)(2,1)S(1)} custom-call(bf16[64,8192]{1,0:T(8,128)(2,1)S(1)} %copy-done, bf16[64,128]{1,0:T(8,128)(2,1)S(1)} %collective-permute-done.rim_ref, f32[64,64]{1,0:T(8,128)S(1)} %copy-done.1), custom_call_target="tpu_custom_call" | custom-call | tf_op jit(solution)/shard_map/pallas_call | solution.py:56
  12.8 2.0 %all_gather.3.rows_ref = bf16[128,1152]{1,0:T(8,128)(2,1)S(1)} all-gather(bf16[64,1152]{1,0:T(8,128)(2,1)S(1)} %shard_map.41), channel_id=1, replica_groups=mesh['tm'=16,'chan'=2] {'chan'}, dimensions={0}, use_global_device_ids=true | all-gather | bytes 442368 | tf_op jit(solution)/shard_map/all_gather | solution.py:323
  14.8 0.6 shard_map.42
  15.4 25.8 %shard_map.43.sums_ref = f32[128,1152]{1,0:T(8,128)S(1)} custom-call(f32[128,1152]{1,0:T(8,128)S(1)} %get-tuple-element.4.mine_ref), custom_call_target="tpu_custom_call" | custom-call | tf_op jit(solution)/shard_map/pallas_call | solution.py:191
  41.3 70.9 %shard_map.44 = (f32[32,1024]{1,0:T(8,128)}, bf16[1024,512]{1,0:T(8,128)(2,1)}) custom-call(f32[128,1152]{1,0:T(8,128)S(1)} %shard_map.43.sums_ref, bf16[1024,512]{1,0:T(8,128)(2,1)S(1)} %get-tuple-element.5.hankel_ref), custom_call_target="tpu_custom_call" | custom-call | tf_op jit(solution)/shard_map/pallas_call | solution.py:305
Async XLA Ops:
  0.6 7.3 %copy-start.1 = (f32[64,64]{1,0:T(8,128)S(1)}, f32[64,64]{1,0:T(8,128)}, u32[]{:S(2)}) copy-start(f32[64,64]{1,0:T(8,128)} %taps_ref.1) | copy-start | bytes 49156
  1.4 6.5 %collective-permute-start = (bf16[64,128]{1,0:T(8,128)(2,1)S(1)}, bf16[64,128]{1,0:T(8,128)(2,1)S(1)}, u32[]{:S(2)}, u32[]{:S(2)}) collective-permute-start(bf16[64,128]{1,0:T(8,128)(2,1)S(1)} %slice.3), channel_id=1, source_target_pairs={{2,0},{4,2},{6,4},{8,6},{10,8},{12,10},{14,12},{16,14},{18,16},{20... | collective-permute-start | bytes 49160 | tf_op jit(solution)/shard_map/ppermute | solution.py:22
  7.9 1.2 %copy-start = (bf16[64,8192]{1,0:T(8,128)(2,1)S(1)}, bf16[64,8192]{1,0:T(8,128)(2,1)}, u32[]{:S(2)}) copy-start(bf16[64,8192]{1,0:T(8,128)(2,1)} %strain_ref.1) | copy-start | bytes 3145732

commit v3 on v2

--- a/solution.py
+++ b/solution.py
@@ -246,7 +246,7 @@
     return jnp.where(col_id >= row_id, factor, 0.0), jnp.concatenate(inverses, axis=0)
 
 
-def whiten_kernel(rows_all, sums_ref, hankel_ref, factor_ref, white_ref, work_ref):
+def whiten_kernel(rows_all, sums_ref, hankel_ref, factor_ref, white_ref, work_ref, left_ref, right_ref):
     columns, count = hankel_ref.shape
     channels = columns // LAGS
     size = channels
@@ -276,18 +276,31 @@
         work_ref[mine, mine] = factor
         white_ref[mine, :] = solved[:, columns:].astype(jnp.bfloat16)
 
-        def update(i, _):
+        high = solved.astype(jnp.bfloat16)
+        rest = solved - high.astype(jnp.float32)
+        middle = rest.astype(jnp.bfloat16)
+        little = (rest - middle.astype(jnp.float32)).astype(jnp.bfloat16)
+        for n, (left, right) in enumerate(
+            ((high, high), (high, middle), (middle, high), (middle, middle), (high, little), (little, high))
+        ):
+            left_ref[n * size : (n + 1) * size, :] = left[:, :columns]
+            right_ref[n * size : (n + 1) * size, :] = right
+
+        def update(start, i, _):
             other = pl.ds(pl.multiple_of(i * size, size), size)
-            work_ref[other, :] -= lax.dot_general(
-                work_ref[mine, other],
-                work_ref[mine, :],
+            work_ref[other, start:] -= lax.dot_general(
+                left_ref[:, other],
+                right_ref[:, start:],
                 (((0,), (0,)), ((), ())),
                 preferred_element_type=jnp.float32,
-                precision=HIGHEST,
             )
             return 0
 
-        lax.fori_loop(k + 1, LAGS, update, 0)
+        middle_lag = LAGS // 2
+        lax.fori_loop(k + 1, middle_lag, functools.partial(update, 0), 0)
+        lax.fori_loop(
+            jnp.maximum(k + 1, middle_lag), LAGS, functools.partial(update, middle_lag * size), 0
+        )
         return 0
 
     lax.fori_loop(0, LAGS, step, 0)
@@ -310,7 +323,11 @@
         ),
         in_specs=[VMEM, VMEM],
         out_specs=(VMEM, VMEM),
-        scratch_shapes=[pltpu.VMEM((columns, columns + count), jnp.float32)],
+        scratch_shapes=[
+            pltpu.VMEM((columns, columns + count), jnp.float32),
+            pltpu.VMEM((6 * columns // LAGS, columns), jnp.bfloat16),
+            pltpu.VMEM((6 * columns // LAGS, columns + count), jnp.bfloat16),
+        ],
         compiler_params=pltpu.CompilerParams(vmem_limit_bytes=48 * 2**20),
     )(sums, hankel)
 

time: 112 us -> 102 us (0.911)
  Pallas kernels: 101 us -> 90.8 us
    pallas_call x1, Pallas kernels: 70.9 us -> 60.7 us  [whiten(): pl.pallas_call(functools.partial(whiten_kernel, rows_all), out_shape=(jax...]
where the time goes in v3:
time: 102 us
  Pallas kernels  90.8 us (89%)
  waiting for transfers between devices  5.26 us (5%)
  blocking collectives  2.02 us (2%)
  local copies, waits for them, and re-layouts  1.95 us (2%)
  starting transfers between devices  1.28 us (1%)
    pallas_call x1, Pallas kernels, whiten(): pl.pallas_call(functools.partial(whiten_kernel, rows_all), out_shape=(jax...  60.7 us
    pallas_call x1, Pallas kernels, summed(): pl.pallas_call(functools.partial(sum_kernel, near), out_shape=jax.ShapeDt...  25.8 us
    ppermute x1, waiting for transfers between devices, shifted(): lax.ppermute(value, axis, [(source, source + steps) for source in range(i...  5.26 us
    pallas_call x1, Pallas kernels, decimate(): pl.pallas_call(decimate_kernel, out_shape=jax.ShapeDtypeStruct((channels,...  3.67 us
  transfers between devices with their start and end apart: 1, of which 1 were waited for; matrix products, arithmetic and copies ran while one was open for 0% of the time, Pallas kernels for 0%

profile of v3, /device:TPU:0, one launch (start us, length us, event | category | flops | bytes accessed | tf_op | source)
XLA Modules:
  0.0 101.9 jit_solution(17207546688493097400)
XLA Ops:
  0.6 0.0 copy-start.1
  0.6 0.7 slice.3
  1.4 1.3 %collective-permute-start = (bf16[64,128]{1,0:T(8,128)(2,1)S(1)}, bf16[64,128]{1,0:T(8,128)(2,1)S(1)}, u32[]{:S(2)}, u32[]{:S(2)}) collective-permute-start(bf16[64,128]{1,0:T(8,128)(2,1)S(1)} %slice.3), channel_id=1, source_target_pairs={{2,0},{4,2},{6,4},{8,6},{10,8},{12,10},{14,12},{16,14},{18,16},{20... | collective-permute-start | bytes 49160 | tf_op jit(solution)/shard_map/ppermute | solution.py:22
  2.7 5.3 %collective-permute-done.rim_ref = bf16[64,128]{1,0:T(8,128)(2,1)S(1)} collective-permute-done((bf16[64,128]{1,0:T(8,128)(2,1)S(1)}, bf16[64,128]{1,0:T(8,128)(2,1)S(1)}, u32[]{:S(2)}, u32[]{:S(2)}) %collective-permute-start) | collective-permute-done | bytes 16416 | tf_op jit(solution)/shard_map/ppermute | solution.py:22
  7.9 0.0 copy-done.1
  7.9 0.0 copy-start
  7.9 1.2 %copy-done = bf16[64,8192]{1,0:T(8,128)(2,1)S(1)} copy-done((bf16[64,8192]{1,0:T(8,128)(2,1)S(1)}, bf16[64,8192]{1,0:T(8,128)(2,1)}, u32[]{:S(2)}) %copy-start) | copy-done | bytes 1048600
  9.1 3.7 %shard_map.41 = bf16[64,1152]{1,0:T(8,128)(2,1)S(1)} custom-call(bf16[64,8192]{1,0:T(8,128)(2,1)S(1)} %copy-done, bf16[64,128]{1,0:T(8,128)(2,1)S(1)} %collective-permute-done.rim_ref, f32[64,64]{1,0:T(8,128)S(1)} %copy-done.1), custom_call_target="tpu_custom_call" | custom-call | tf_op jit(solution)/shard_map/pallas_call | solution.py:56
  12.8 2.0 %all_gather.3.rows_ref = bf16[128,1152]{1,0:T(8,128)(2,1)S(1)} all-gather(bf16[64,1152]{1,0:T(8,128)(2,1)S(1)} %shard_map.41), channel_id=1, replica_groups=mesh['tm'=16,'chan'=2] {'chan'}, dimensions={0}, use_global_device_ids=true | all-gather | bytes 442368 | tf_op jit(solution)/shard_map/all_gather | solution.py:340
  14.8 0.6 shard_map.42
  15.4 25.8 %shard_map.43.sums_ref = f32[128,1152]{1,0:T(8,128)S(1)} custom-call(f32[128,1152]{1,0:T(8,128)S(1)} %get-tuple-element.4.mine_ref), custom_call_target="tpu_custom_call" | custom-call | tf_op jit(solution)/shard_map/pallas_call | solution.py:191
  41.3 60.7 %shard_map.44 = (f32[32,1024]{1,0:T(8,128)}, bf16[1024,512]{1,0:T(8,128)(2,1)}) custom-call(f32[128,1152]{1,0:T(8,128)S(1)} %shard_map.43.sums_ref, bf16[1024,512]{1,0:T(8,128)(2,1)S(1)} %get-tuple-element.5.hankel_ref), custom_call_target="tpu_custom_call" | custom-call | tf_op jit(solution)/shard_map/pallas_call | solution.py:318
Async XLA Ops:
  0.6 7.3 %copy-start.1 = (f32[64,64]{1,0:T(8,128)S(1)}, f32[64,64]{1,0:T(8,128)}, u32[]{:S(2)}) copy-start(f32[64,64]{1,0:T(8,128)} %taps_ref.1) | copy-start | bytes 49156
  1.4 6.5 %collective-permute-start = (bf16[64,128]{1,0:T(8,128)(2,1)S(1)}, bf16[64,128]{1,0:T(8,128)(2,1)S(1)}, u32[]{:S(2)}, u32[]{:S(2)}) collective-permute-start(bf16[64,128]{1,0:T(8,128)(2,1)S(1)} %slice.3), channel_id=1, source_target_pairs={{2,0},{4,2},{6,4},{8,6},{10,8},{12,10},{14,12},{16,14},{18,16},{20... | collective-permute-start | bytes 49160 | tf_op jit(solution)/shard_map/ppermute | solution.py:22
  7.9 1.2 %copy-start = (bf16[64,8192]{1,0:T(8,128)(2,1)S(1)}, bf16[64,8192]{1,0:T(8,128)(2,1)}, u32[]{:S(2)}) copy-start(bf16[64,8192]{1,0:T(8,128)(2,1)} %strain_ref.1) | copy-start | bytes 3145732

commit v4 on v3

--- a/solution.py
+++ b/solution.py
@@ -296,11 +296,9 @@
             )
             return 0
 
-        middle_lag = LAGS // 2
-        lax.fori_loop(k + 1, middle_lag, functools.partial(update, 0), 0)
-        lax.fori_loop(
-            jnp.maximum(k + 1, middle_lag), LAGS, functools.partial(update, middle_lag * size), 0
-        )
+        for q in range(0, LAGS, 2):
+            initial, last = jnp.maximum(k + 1, q), jnp.maximum(k + 1, q + 2)
+            lax.fori_loop(initial, last, functools.partial(update, q * size), 0)
         return 0
 
     lax.fori_loop(0, LAGS, step, 0)

time: 102 us -> 102 us (level)
  no operation moved by 1% of the time
where the time goes in v4:
time: 102 us; the launch traced here: 101 us
  Pallas kernels  90.1 us (88%)
  waiting for transfers between devices  5.26 us (5%)
  blocking collectives  2.02 us (2%)
  local copies, waits for them, and re-layouts  1.95 us (2%)
  starting transfers between devices  1.28 us (1%)
    pallas_call x1, Pallas kernels, whiten(): pl.pallas_call(functools.partial(whiten_kernel, rows_all), out_shape=(jax...  60 us
    pallas_call x1, Pallas kernels, summed(): pl.pallas_call(functools.partial(sum_kernel, near), out_shape=jax.ShapeDt...  25.8 us
    ppermute x1, waiting for transfers between devices, shifted(): lax.ppermute(value, axis, [(source, source + steps) for source in range(i...  5.26 us
    pallas_call x1, Pallas kernels, decimate(): pl.pallas_call(decimate_kernel, out_shape=jax.ShapeDtypeStruct((channels,...  3.67 us
  transfers between devices with their start and end apart: 1, of which 1 were waited for; matrix products, arithmetic and copies ran while one was open for 0% of the time, Pallas kernels for 0%

profile of v4, /device:TPU:0, one launch (start us, length us, event | category | flops | bytes accessed | tf_op | source)
XLA Modules:
  0.0 101.3 jit_solution(8896548324422320221)
XLA Ops:
  0.6 0.0 copy-start.1
  0.6 0.7 slice.3
  1.4 1.3 %collective-permute-start = (bf16[64,128]{1,0:T(8,128)(2,1)S(1)}, bf16[64,128]{1,0:T(8,128)(2,1)S(1)}, u32[]{:S(2)}, u32[]{:S(2)}) collective-permute-start(bf16[64,128]{1,0:T(8,128)(2,1)S(1)} %slice.3), channel_id=1, source_target_pairs={{2,0},{4,2},{6,4},{8,6},{10,8},{12,10},{14,12},{16,14},{18,16},{20... | collective-permute-start | bytes 49160 | tf_op jit(solution)/shard_map/ppermute | solution.py:22
  2.7 5.3 %collective-permute-done.rim_ref = bf16[64,128]{1,0:T(8,128)(2,1)S(1)} collective-permute-done((bf16[64,128]{1,0:T(8,128)(2,1)S(1)}, bf16[64,128]{1,0:T(8,128)(2,1)S(1)}, u32[]{:S(2)}, u32[]{:S(2)}) %collective-permute-start) | collective-permute-done | bytes 16416 | tf_op jit(solution)/shard_map/ppermute | solution.py:22
  7.9 0.0 copy-done.1
  7.9 0.0 copy-start
  7.9 1.2 %copy-done = bf16[64,8192]{1,0:T(8,128)(2,1)S(1)} copy-done((bf16[64,8192]{1,0:T(8,128)(2,1)S(1)}, bf16[64,8192]{1,0:T(8,128)(2,1)}, u32[]{:S(2)}) %copy-start) | copy-done | bytes 1048600
  9.1 3.7 %shard_map.41 = bf16[64,1152]{1,0:T(8,128)(2,1)S(1)} custom-call(bf16[64,8192]{1,0:T(8,128)(2,1)S(1)} %copy-done, bf16[64,128]{1,0:T(8,128)(2,1)S(1)} %collective-permute-done.rim_ref, f32[64,64]{1,0:T(8,128)S(1)} %copy-done.1), custom_call_target="tpu_custom_call" | custom-call | tf_op jit(solution)/shard_map/pallas_call | solution.py:56
  12.8 2.0 %all_gather.3.rows_ref = bf16[128,1152]{1,0:T(8,128)(2,1)S(1)} all-gather(bf16[64,1152]{1,0:T(8,128)(2,1)S(1)} %shard_map.41), channel_id=1, replica_groups=mesh['tm'=16,'chan'=2] {'chan'}, dimensions={0}, use_global_device_ids=true | all-gather | bytes 442368 | tf_op jit(solution)/shard_map/all_gather | solution.py:338
  14.8 0.6 shard_map.42
  15.4 25.8 %shard_map.43.sums_ref = f32[128,1152]{1,0:T(8,128)S(1)} custom-call(f32[128,1152]{1,0:T(8,128)S(1)} %get-tuple-element.4.mine_ref), custom_call_target="tpu_custom_call" | custom-call | tf_op jit(solution)/shard_map/pallas_call | solution.py:191
  41.3 60.0 %shard_map.44 = (f32[32,1024]{1,0:T(8,128)}, bf16[1024,512]{1,0:T(8,128)(2,1)}) custom-call(f32[128,1152]{1,0:T(8,128)S(1)} %shard_map.43.sums_ref, bf16[1024,512]{1,0:T(8,128)(2,1)S(1)} %get-tuple-element.5.hankel_ref), custom_call_target="tpu_custom_call" | custom-call | tf_op jit(solution)/shard_map/pallas_call | solution.py:316
Async XLA Ops:
  0.6 7.3 %copy-start.1 = (f32[64,64]{1,0:T(8,128)S(1)}, f32[64,64]{1,0:T(8,128)}, u32[]{:S(2)}) copy-start(f32[64,64]{1,0:T(8,128)} %taps_ref.1) | copy-start | bytes 49156
  1.4 6.5 %collective-permute-start = (bf16[64,128]{1,0:T(8,128)(2,1)S(1)}, bf16[64,128]{1,0:T(8,128)(2,1)S(1)}, u32[]{:S(2)}, u32[]{:S(2)}) collective-permute-start(bf16[64,128]{1,0:T(8,128)(2,1)S(1)} %slice.3), channel_id=1, source_target_pairs={{2,0},{4,2},{6,4},{8,6},{10,8},{12,10},{14,12},{16,14},{18,16},{20... | collective-permute-start | bytes 49160 | tf_op jit(solution)/shard_map/ppermute | solution.py:22
  7.9 1.2 %copy-start = (bf16[64,8192]{1,0:T(8,128)(2,1)S(1)}, bf16[64,8192]{1,0:T(8,128)(2,1)}, u32[]{:S(2)}) copy-start(bf16[64,8192]{1,0:T(8,128)(2,1)} %strain_ref.1) | copy-start | bytes 3145732
